TPU v7x, 256 devices: a whole 4x4x8 slice. The times are simulated.
256 devices in a mesh: row: 32 (over y, z_lo, core), col: 8 (over z_hi, x).
Axes of the slice: x: 4, y: 4, z: 8 (z_hi: 2, z_lo: 4; z = z_hi * 4 + z_lo), core: 2. Of those that a mesh axis runs over, the one named last changes fastest.
Arguments:
- views: bfloat16 [81, 2048, 2048], P(None, 'row', 'col'), may hold values from -6 to 6
Outputs:
- increment: float32 [2048, 2048], P('row', 'col')
- residual: float32 [2048, 2048], P('row', 'col')
All inputs are finite; a program needn't handle non-finite values.
Results may differ from a plain program's by a relative error of at most 0.0005.
Values may be sent and summed in bfloat16 or wider, within the bound.
No kernel may reach another device: no remote copies, remote signals or barrier semaphores. Data moves between devices by JAX's collectives and lax.ppermute only.
A program may use at most 64 MiB of HBM per device.

v0:
```python
import jax
import jax.numpy as jnp
from jax import lax
from jax.sharding import Mesh
from jax.sharding import PartitionSpec as P

ANG = 9
VIEWS = 81
D0 = 3
HALO = 13
ITERS = 2
ROW_COL = ("row_0", "row_1", "row_2", "col_0", "col_1")
ROW = ("row_0", "row_1", "row_2")
COL = ("col_0", "col_1")
smooth_weight = 2.0
damping = 0.1


def with_halo(array, sides, width):
    for axis, dim in sides:
        count, length = (lax.axis_size(axis), array.shape[dim])
        up = [(i, (i + 1) % count) for i in range(count - 1)]
        down = [(j, i) for i, j in up]
        last = lax.slice_in_dim(array, length - width, length, axis=dim)
        leading = lax.slice_in_dim(array, 0, width, axis=dim)
        before = lax.ppermute(last, axis, up)
        after = lax.ppermute(leading, axis, down)
        array = jnp.concatenate([before, array, after], axis=dim)
    return array


def by_axis(array, axes):
    for axis in axes:
        array = lax.psum(array, axis)
    return array


def operate(field, coeff, horiz, verti):
    padded = with_halo(field, ((ROW, 0), (COL, 1)), 1)
    edges = horiz[:, 1:] * (field - padded[1:-1, 2:]) + horiz[:, :-1] * (field - padded[1:-1, :-2])
    edges = (
        edges + verti[1:] * (field - padded[2:, 1:-1]) + verti[:-1] * (field - padded[:-2, 1:-1])
    )
    return coeff * field + smooth_weight * edges


def row_band(col_ext, srow_index, rows_dev):
    srow = srow_index - ANG // 2
    reach = D0 * abs(srow) + 1
    block = col_ext[srow_index * ANG : (srow_index + 1) * ANG]
    grown = with_halo(block, ((ROW, 1),), reach)
    start = reach + D0 * srow - 1
    return grown[:, start : start + rows_dev + 2, :]


def shards(views):
    rows_dev = views.shape[1]
    cols_dev = views.shape[2]
    total_rows = rows_dev * lax.axis_size(ROW)
    total_cols = cols_dev * lax.axis_size(COL)
    bands = []
    col_ext = with_halo(views, ((COL, 2),), HALO)
    for srow_index in range(ANG):
        bands.append(row_band(col_ext, srow_index, rows_dev))
    center_ext = bands[ANG // 2][ANG // 2, :, HALO - 1 : HALO + cols_dev + 1].astype(jnp.float32)
    center = center_ext[1:-1, 1:-1]
    data_sum = jnp.zeros((rows_dev, cols_dev), jnp.float32)
    source_sum = jnp.zeros((rows_dev, cols_dev), jnp.float32)
    for srow_index in range(ANG):
        srow = float(srow_index - ANG // 2)
        band = bands[srow_index]
        for tindex in range(ANG):
            tcol = tindex - ANG // 2
            left = HALO + D0 * tcol
            image = band[tindex].astype(jnp.float32)
            warped = image[1:-1, left : left + cols_dev]
            down_diff = 0.5 * (
                image[2:, left : left + cols_dev] - image[:-2, left : left + cols_dev]
            )
            side_diff = 0.5 * (
                image[1:-1, left + 1 : left + 1 + cols_dev]
                - image[1:-1, left - 1 : left - 1 + cols_dev]
            )
            slope = srow * down_diff + tcol * side_diff
            error = warped - center
            robust = 1.0 / jnp.sqrt(1.0 + error * error)
            data_sum = data_sum + robust * slope * slope
            source_sum = source_sum - robust * slope * error
    coeff = damping + data_sum / VIEWS
    source = source_sum / VIEWS
    across = center_ext[1:-1, 1:] - center_ext[1:-1, :-1]
    vertical = center_ext[1:, 1:-1] - center_ext[:-1, 1:-1]
    columns = lax.axis_index(COL) * cols_dev + jnp.arange(cols_dev + 1)
    row_index = lax.axis_index(ROW) * rows_dev + jnp.arange(rows_dev + 1)
    horiz = jnp.where(
        ((columns >= 1) & (columns <= total_cols - 1))[None, :], jnp.exp(-across * across), 0.0
    )
    verti = jnp.where(
        ((row_index >= 1) & (row_index <= total_rows - 1))[:, None],
        jnp.exp(-vertical * vertical),
        0.0,
    )
    precond = coeff + smooth_weight * (horiz[:, 1:] + horiz[:, :-1] + verti[1:] + verti[:-1])
    solution = jnp.zeros_like(source)
    residual = source
    scaled_res = residual / precond
    image_res = operate(scaled_res, coeff, horiz, verti)
    inner_old = None
    step_old = None
    for step in range(ITERS):
        inner_rz, inner_wu = (
            by_axis(jnp.sum(residual * scaled_res), ROW_COL),
            by_axis(jnp.sum(image_res * scaled_res), ROW_COL),
        )
        scaled_img = image_res / precond
        last_step = step + 1 == ITERS
        if not last_step:
            next_image = operate(scaled_img, coeff, horiz, verti)
        if step == 0:
            step_size = inner_rz / inner_wu
            direction = scaled_res
            dir_image = image_res
            dir_scaled = scaled_img
            dir_second = next_image
        else:
            momentum = inner_rz / inner_old
            step_size = inner_rz / (inner_wu - momentum * inner_rz / step_old)
            direction = scaled_res + momentum * direction
            dir_image = image_res + momentum * dir_image
        solution = solution + step_size * direction
        residual = residual - step_size * dir_image
        if not last_step:
            scaled_res = scaled_res - step_size * dir_scaled
            image_res = image_res - step_size * dir_second
        inner_old = inner_rz
        step_old = step_size
    return (solution, residual)


def solution(mesh):
    finer = Mesh(mesh.devices.reshape(4, 4, 2, 2, 4), ("row_0", "row_1", "row_2", "col_0", "col_1"))
    in_specs = (P(None, ROW, COL),)
    out_specs = (P(ROW, COL), P(ROW, COL))
    return jax.shard_map(
        shards, mesh=finer, in_specs=in_specs, out_specs=out_specs, check_vma=False
    )
```

profile of v0, /device:TPU:10, one launch (start us, length us, event | category | flops | bytes accessed | tf_op | source)
XLA Modules:
  0.0 256.1 jit_solution(15290785969575630049)
XLA Ops:
  0.6 3.4 %fusion.427 = (bf16[81,64,13]{2,1,0:T(8,128)(2,1)}, bf16[81,64,13]{2,1,0:T(8,128)(2,1)S(1)}) fusion(bf16[81,64,256]{2,1,0:T(8,128)(2,1)} %param.1), kind=kLoop, calls=%fused_computation.861 | loop fusion | bytes 539136 | tf_op jit(solution)/shard_map/slice | solution.py:24
  5.8 2.7 %collective-permute-start.1 = (bf16[81,64,13]{0,1,2:T(8,128)(2,1)S(1)}, bf16[81,64,13]{0,1,2:T(8,128)(2,1)S(1)}, u32[]{:S(2)}, u32[]{:S(2)}) collective-permute-start(bf16[81,64,13]{0,1,2:T(8,128)(2,1)S(1)} %copy.8), channel_id=1, source_target_pairs={{1,0},{2,1},{3,2},{4,3},{5,4},{6,5},{7,6},{9,8},{10,9},{11,10},{12... | collective-permute-start | bytes 404360 | tf_op jit(solution)/shard_map/ppermute | solution.py:27
  8.5 2.9 %copy.7 = bf16[81,64,13]{0,1,2:T(8,128)(2,1)S(1)} copy(bf16[81,64,13]{2,1,0:T(8,128)(2,1)} %get-tuple-element.132) | data formatting | bytes 269568
  11.4 3.4 %collective-permute-start = (bf16[81,64,13]{0,1,2:T(8,128)(2,1)S(1)}, bf16[81,64,13]{0,1,2:T(8,128)(2,1)S(1)}, u32[]{:S(2)}, u32[]{:S(2)}) collective-permute-start(bf16[81,64,13]{0,1,2:T(8,128)(2,1)S(1)} %copy.7), channel_id=1, source_target_pairs={{0,1},{1,2},{2,3},{3,4},{4,5},{5,6},{6,7},{8,9},{9,10},{10,11},{11... | collective-permute-start | bytes 404360 | tf_op jit(solution)/shard_map/ppermute | solution.py:26
  14.8 5.2 %collective-permute-done = bf16[81,64,13]{0,1,2:T(8,128)(2,1)S(1)} collective-permute-done((bf16[81,64,13]{0,1,2:T(8,128)(2,1)S(1)}, bf16[81,64,13]{0,1,2:T(8,128)(2,1)S(1)}, u32[]{:S(2)}, u32[]{:S(2)}) %collective-permute-start) | collective-permute-done | bytes 134816 | tf_op jit(solution)/shard_map/ppermute | solution.py:26
  20.0 3.2 %copy.5 = bf16[81,64,13]{2,1,0:T(8,128)(2,1)} copy(bf16[81,64,13]{0,1,2:T(8,128)(2,1)S(1)} %collective-permute-done) | data formatting | bytes 269568 | tf_op jit(solution)/shard_map/ppermute | solution.py:26
  23.2 3.2 %copy.6 = bf16[81,64,13]{2,1,0:T(8,128)(2,1)} copy(bf16[81,64,13]{0,1,2:T(8,128)(2,1)S(1)} %collective-permute-done.1) | data formatting | bytes 269568 | tf_op jit(solution)/shard_map/ppermute | solution.py:27
  28.6 2.8 %pad_maximum_fusion = bf16[81,64,282]{2,1,0:T(8,128)(2,1)S(1)} fusion(bf16[81,64,13]{2,1,0:T(8,128)(2,1)S(1)} %copy-done.2, bf16[81,64,256]{2,1,0:T(8,128)(2,1)S(1)} %copy-done, bf16[81,64,13]{2,1,0:T(8,128)(2,1)S(1)} %copy-done.1), kind=kLoop, calls=%fused_computation | loop fusion | flops 8771328 | bytes 5847552 | tf_op jit(solution)/shard_map/concatenate | solution.py:28
  33.3 6.3 %collective-permute-start.4 = (bf16[9,1,282]{2,1,0:T(2,128)(2,1)S(1)}, bf16[9,1,282]{2,1,0:T(2,128)(2,1)S(1)}, u32[]{:S(2)}, u32[]{:S(2)}) collective-permute-start(bf16[9,1,282]{2,1,0:T(2,128)(2,1)S(1)} %get-tuple-element.122), channel_id=1, source_target_pairs={{8,0},{16,8},{24,16},{32,24},{40,32},{48,40},{56,48},{64,56},{72,6... | collective-permute-start | bytes 15236 | tf_op jit(solution)/shard_map/ppermute | solution.py:27
  39.7 2.1 collective-permute-start.8
  41.8 2.2 collective-permute-start.7
  44.0 6.0 %collective-permute-start.9 = (bf16[9,7,282]{2,1,0:T(8,128)(2,1)S(1)}, bf16[9,7,282]{2,1,0:T(8,128)(2,1)S(1)}, u32[]{:S(2)}, u32[]{:S(2)}) collective-permute-start(bf16[9,7,282]{2,1,0:T(8,128)(2,1)S(1)} %get-tuple-element.117), channel_id=1, source_target_pairs={{8,0},{16,8},{24,16},{32,24},{40,32},{48,40},{56,48},{64,56},{72,6... | collective-permute-start | bytes 106604 | tf_op jit(solution)/shard_map/ppermute | solution.py:27
  52.8 6.3 %collective-permute-start.10 = (bf16[9,10,282]{2,1,0:T(8,128)(2,1)S(1)}, bf16[9,10,282]{2,1,0:T(8,128)(2,1)S(1)}, u32[]{:S(2)}, u32[]{:S(2)}) collective-permute-start(bf16[9,10,282]{2,1,0:T(8,128)(2,1)S(1)} %get-tuple-element.115), channel_id=1, source_target_pairs={{8,0},{16,8},{24,16},{32,24},{40,32},{48,40},{56,48},{64,56},{72,6... | collective-permute-start | bytes 152288 | tf_op jit(solution)/shard_map/ppermute | solution.py:27
  61.8 6.3 %collective-permute-start.11 = (bf16[9,13,282]{2,1,0:T(8,128)(2,1)S(1)}, bf16[9,13,282]{2,1,0:T(8,128)(2,1)S(1)}, u32[]{:S(2)}, u32[]{:S(2)}) collective-permute-start(bf16[9,13,282]{2,1,0:T(8,128)(2,1)S(1)} %get-tuple-element.113), channel_id=1, source_target_pairs={{8,0},{16,8},{24,16},{32,24},{40,32},{48,40},{56,48},{64,56},{72,6... | collective-permute-start | bytes 197972 | tf_op jit(solution)/shard_map/ppermute | solution.py:27
  68.3 2.1 collective-permute-start.2
  78.1 27.1 %subtract_multiply_fusion = (f32[64,256]{1,0:T(8,128)}, f32[64,256]{1,0:T(8,128)}, f32[64,256]{1,0:T(8,128)}, f32[64,256]{1,0:T(8,128)}, f32[64,256]{1,0:T(8,128...) fusion(f32[66,282]{1,0:T(8,128)} %get-tuple-element.169, ...), kind=kLoop, calls=%fused_computation.594 | loop fusion | flops 14188544 | bytes 31981568 | tf_op jit(solution)/shard_map/div | solution.py:90
  105.2 7.2 %fusion.344 = (f32[64,256]{1,0:T(8,128)S(1)}, f32[64,256]{1,0:T(8,128)S(1)}, f32[64,256]{1,0:T(8,128)S(1)}) fusion(f32[64,256]{1,0:T(8,128)} %get-tuple-element.31, f32[65,256]{1,0:T(8,128)S(1)} %fusion.3, f32[64,257]{1,0:T(8,128)S(1)} %fusion.1, f32[64,256]{1,0:T(8,128)} %get-tuple-element.112, f32[66,282]{1,0:T(8,128)} %get-tuple-element.134, ...), kind=kLoop, calls=%fused_computation.859 | loop fusion | flops 8077312 | bytes 11206656 | tf_op jit(solution)/shard_map/div | solution.py:106
  112.5 4.6 %collective-permute-start.13 = (f32[1,256]{1,0:T(1,128)S(1)}, f32[1,256]{1,0:T(1,128)S(1)}, u32[]{:S(2)}, u32[]{:S(2)}) collective-permute-start(f32[1,256]{1,0:T(1,128)S(1)} %get-tuple-element.221), channel_id=1, source_target_pairs={{8,0},{16,8},{24,16},{32,24},{40,32},{48,40},{56,48},{64,56},{72,6... | collective-permute-start | bytes 3080 | tf_op jit(solution)/shard_map/ppermute | solution.py:27
  119.0 5.6 %collective-permute-done.12 = f32[1,256]{1,0:T(1,128)S(1)} collective-permute-done((f32[1,256]{1,0:T(1,128)S(1)}, f32[1,256]{1,0:T(1,128)S(1)}, u32[]{:S(2)}, u32[]{:S(2)}) %collective-permute-start.12) | collective-permute-done | bytes 1056 | tf_op jit(solution)/shard_map/ppermute | solution.py:26
  126.7 3.9 %collective-permute-start.15 = (f32[66,1]{1,0:T(8,128)S(1)}, f32[66,1]{1,0:T(8,128)S(1)}, u32[]{:S(2)}, u32[]{:S(2)}) collective-permute-start(f32[66,1]{1,0:T(8,128)S(1)} %get-tuple-element.218), channel_id=1, source_target_pairs={{0,1},{1,2},{2,3},{3,4},{4,5},{5,6},{6,7},{8,9},{9,10},{10,11},{11... | collective-permute-start | bytes 800 | tf_op jit(solution)/shard_map/ppermute | solution.py:26
  135.2 2.4 collective-permute-start.16
  137.6 9.3 %all-reduce.5 = (f32[]{:T(128)}, f32[]{:T(128)}) all-reduce(f32[]{:T(128)} %get-tuple-element.5, f32[]{:T(128)} %get-tuple-element.4), channel_id=1, replica_groups=mesh['row_0'=4,'row_1'=4,'row_2'=2,'col_0'=2,'col_1'=4] {'row_0'}, use_global_device_ids=true, to_apply=%region_1.2 | all-reduce | flops 2 | bytes 16 | tf_op jit(solution)/shard_map/psum | solution.py:34
  146.9 9.0 %all-reduce.3 = (f32[]{:T(128)}, f32[]{:T(128)}) all-reduce(f32[]{:T(128)} %get-tuple-element.16, f32[]{:T(128)} %get-tuple-element.17), channel_id=1, replica_groups=mesh['row_0'=4,'row_1'=4,'row_2'=2,'col_0'=2,'col_1'=4] {'row_1'}, use_global_device_ids=true, to_apply=%region_2.3 | all-reduce | flops 2 | bytes 16 | tf_op jit(solution)/shard_map/psum | solution.py:34
  155.9 3.2 %all-reduce.9 = (f32[]{:T(128)}, f32[]{:T(128)}) all-reduce(f32[]{:T(128)} %get-tuple-element.12, f32[]{:T(128)} %get-tuple-element.13), channel_id=1, replica_groups=mesh['row_0'=4,'row_1'=4,'row_2'=2,'col_0'=2,'col_1'=4] {'row_2'}, use_global_device_ids=true, to_apply=%region_3.4 | all-reduce | flops 2 | bytes 16 | tf_op jit(solution)/shard_map/psum | solution.py:34
  159.2 17.8 %all-reduce.7 = (f32[]{:T(128)}, f32[]{:T(128)}) all-reduce(f32[]{:T(128)} %get-tuple-element.24, f32[]{:T(128)} %get-tuple-element.25), channel_id=1, replica_groups=mesh['row_0'=4,'row_1'=4,'row_2'=2,'col_0'=2,'col_1'=4] {'col_0'}, use_global_device_ids=true, to_apply=%region_4.5 | all-reduce | flops 2 | bytes 16 | tf_op jit(solution)/shard_map/psum | solution.py:34
  177.0 7.9 %collective-permute-start.18 = (f32[66,1]{1,0:T(8,128)S(1)}, f32[66,1]{1,0:T(8,128)S(1)}, u32[]{:S(2)}, u32[]{:S(2)}) collective-permute-start(f32[66,1]{1,0:T(8,128)S(1)} %get-tuple-element.215), channel_id=1, source_target_pairs={{1,0},{2,1},{3,2},{4,3},{5,4},{6,5},{7,6},{9,8},{10,9},{11,10},{12... | collective-permute-start | bytes 800 | tf_op jit(solution)/shard_map/ppermute | solution.py:27
  186.9 13.7 %all-reduce.1 = (f32[]{:T(128)}, f32[]{:T(128)}) all-reduce(f32[]{:T(128)} %get-tuple-element.20, f32[]{:T(128)} %get-tuple-element.21), channel_id=1, replica_groups=mesh['row_0'=4,'row_1'=4,'row_2'=2,'col_0'=2,'col_1'=4] {'col_1'}, use_global_device_ids=true, to_apply=%region_5.6 | all-reduce | flops 2 | bytes 16 | tf_op jit(solution)/shard_map/psum | solution.py:34
  203.7 11.0 %all-reduce.4 = (f32[]{:T(128)}, f32[]{:T(128)}) all-reduce(f32[]{:T(128)} %get-tuple-element.3, f32[]{:T(128)} %get-tuple-element.2), channel_id=1, replica_groups=mesh['row_0'=4,'row_1'=4,'row_2'=2,'col_0'=2,'col_1'=4] {'row_0'}, use_global_device_ids=true, to_apply=%region_13.14 | all-reduce | flops 2 | bytes 16 | tf_op jit(solution)/shard_map/psum | solution.py:34
  214.8 11.0 %all-reduce.2 = (f32[]{:T(128)}, f32[]{:T(128)}) all-reduce(f32[]{:T(128)} %get-tuple-element.14, f32[]{:T(128)} %get-tuple-element.15), channel_id=1, replica_groups=mesh['row_0'=4,'row_1'=4,'row_2'=2,'col_0'=2,'col_1'=4] {'row_1'}, use_global_device_ids=true, to_apply=%region_14.15 | all-reduce | flops 2 | bytes 16 | tf_op jit(solution)/shard_map/psum | solution.py:34
  225.8 3.1 %all-reduce.8 = (f32[]{:T(128)}, f32[]{:T(128)}) all-reduce(f32[]{:T(128)} %get-tuple-element.10, f32[]{:T(128)} %get-tuple-element.11), channel_id=1, replica_groups=mesh['row_0'=4,'row_1'=4,'row_2'=2,'col_0'=2,'col_1'=4] {'row_2'}, use_global_device_ids=true, to_apply=%region_15.16 | all-reduce | flops 2 | bytes 16 | tf_op jit(solution)/shard_map/psum | solution.py:34
  228.9 9.5 %all-reduce.6 = (f32[]{:T(128)}, f32[]{:T(128)}) all-reduce(f32[]{:T(128)} %get-tuple-element.22, f32[]{:T(128)} %get-tuple-element.23), channel_id=1, replica_groups=mesh['row_0'=4,'row_1'=4,'row_2'=2,'col_0'=2,'col_1'=4] {'col_0'}, use_global_device_ids=true, to_apply=%region_16.17 | all-reduce | flops 2 | bytes 16 | tf_op jit(solution)/shard_map/psum | solution.py:34
  238.3 11.6 %all-reduce = (f32[]{:T(128)}, f32[]{:T(128)}) all-reduce(f32[]{:T(128)} %get-tuple-element.18, f32[]{:T(128)} %get-tuple-element.19), channel_id=1, replica_groups=mesh['row_0'=4,'row_1'=4,'row_2'=2,'col_0'=2,'col_1'=4] {'col_1'}, use_global_device_ids=true, to_apply=%region_17.18 | all-reduce | flops 2 | bytes 16 | tf_op jit(solution)/shard_map/psum | solution.py:34
  (67 shorter events, 32.7 us)
Async XLA Ops:
  5.8 20.6 %copy-start = (bf16[81,64,256]{2,1,0:T(8,128)(2,1)S(1)}, bf16[81,64,256]{2,1,0:T(8,128)(2,1)}, u32[]{:S(2)}) copy-start(bf16[81,64,256]{2,1,0:T(8,128)(2,1)} %param.1) | copy-start | bytes 7962628
  5.8 17.4 %collective-permute-start.1 = (bf16[81,64,13]{0,1,2:T(8,128)(2,1)S(1)}, bf16[81,64,13]{0,1,2:T(8,128)(2,1)S(1)}, u32[]{:S(2)}, u32[]{:S(2)}) collective-permute-start(bf16[81,64,13]{0,1,2:T(8,128)(2,1)S(1)} %copy.8), channel_id=1, source_target_pairs={{1,0},{2,1},{3,2},{4,3},{5,4},{6,5},{7,6},{9,8},{10,9},{11,10},{12... | collective-permute-start | bytes 404360 | tf_op jit(solution)/shard_map/ppermute | solution.py:27
  11.4 8.6 %collective-permute-start = (bf16[81,64,13]{0,1,2:T(8,128)(2,1)S(1)}, bf16[81,64,13]{0,1,2:T(8,128)(2,1)S(1)}, u32[]{:S(2)}, u32[]{:S(2)}) collective-permute-start(bf16[81,64,13]{0,1,2:T(8,128)(2,1)S(1)} %copy.7), channel_id=1, source_target_pairs={{0,1},{1,2},{2,3},{3,4},{4,5},{5,6},{6,7},{8,9},{9,10},{10,11},{11... | collective-permute-start | bytes 404360 | tf_op jit(solution)/shard_map/ppermute | solution.py:26
  26.4 1.4 copy-start.1
  26.4 1.8 copy-start.2
  31.4 19.5 %collective-permute-start.3 = (bf16[9,1,282]{2,1,0:T(2,128)(2,1)S(1)}, bf16[9,1,282]{2,1,0:T(2,128)(2,1)S(1)}, u32[]{:S(2)}, u32[]{:S(2)}) collective-permute-start(bf16[9,1,282]{2,1,0:T(2,128)(2,1)S(1)} %get-tuple-element.121), channel_id=1, source_target_pairs={{0,8},{8,16},{16,24},{24,32},{32,40},{40,48},{48,56},{56,64},{64,7... | collective-permute-start | bytes 15236 | tf_op jit(solution)/shard_map/ppermute | solution.py:26
  33.3 19.5 %collective-permute-start.4 = (bf16[9,1,282]{2,1,0:T(2,128)(2,1)S(1)}, bf16[9,1,282]{2,1,0:T(2,128)(2,1)S(1)}, u32[]{:S(2)}, u32[]{:S(2)}) collective-permute-start(bf16[9,1,282]{2,1,0:T(2,128)(2,1)S(1)} %get-tuple-element.122), channel_id=1, source_target_pairs={{8,0},{16,8},{24,16},{32,24},{40,32},{48,40},{56,48},{64,56},{72,6... | collective-permute-start | bytes 15236 | tf_op jit(solution)/shard_map/ppermute | solution.py:27
  39.7 20.1 %collective-permute-start.8 = (bf16[9,4,282]{2,1,0:T(4,128)(2,1)S(1)}, bf16[9,4,282]{2,1,0:T(4,128)(2,1)S(1)}, u32[]{:S(2)}, u32[]{:S(2)}) collective-permute-start(bf16[9,4,282]{2,1,0:T(4,128)(2,1)S(1)} %get-tuple-element.119), channel_id=1, source_target_pairs={{8,0},{16,8},{24,16},{32,24},{40,32},{48,40},{56,48},{64,56},{72,6... | collective-permute-start | bytes 60920 | tf_op jit(solution)/shard_map/ppermute | solution.py:27
  41.8 20.0 %collective-permute-start.7 = (bf16[9,4,282]{2,1,0:T(4,128)(2,1)S(1)}, bf16[9,4,282]{2,1,0:T(4,128)(2,1)S(1)}, u32[]{:S(2)}, u32[]{:S(2)}) collective-permute-start(bf16[9,4,282]{2,1,0:T(4,128)(2,1)S(1)} %get-tuple-element.120), channel_id=1, source_target_pairs={{0,8},{8,16},{16,24},{24,32},{32,40},{40,48},{48,56},{56,64},{64,7... | collective-permute-start | bytes 60920 | tf_op jit(solution)/shard_map/ppermute | solution.py:26
  44.0 27.3 %collective-permute-start.9 = (bf16[9,7,282]{2,1,0:T(8,128)(2,1)S(1)}, bf16[9,7,282]{2,1,0:T(8,128)(2,1)S(1)}, u32[]{:S(2)}, u32[]{:S(2)}) collective-permute-start(bf16[9,7,282]{2,1,0:T(8,128)(2,1)S(1)} %get-tuple-element.117), channel_id=1, source_target_pairs={{8,0},{16,8},{24,16},{32,24},{40,32},{48,40},{56,48},{64,56},{72,6... | collective-permute-start | bytes 106604 | tf_op jit(solution)/shard_map/ppermute | solution.py:27
  50.9 17.4 %collective-permute-start.6 = (bf16[9,7,282]{2,1,0:T(8,128)(2,1)S(1)}, bf16[9,7,282]{2,1,0:T(8,128)(2,1)S(1)}, u32[]{:S(2)}, u32[]{:S(2)}) collective-permute-start(bf16[9,7,282]{2,1,0:T(8,128)(2,1)S(1)} %get-tuple-element.118), channel_id=1, source_target_pairs={{0,8},{8,16},{16,24},{24,32},{32,40},{40,48},{48,56},{56,64},{64,7... | collective-permute-start | bytes 106604 | tf_op jit(solution)/shard_map/ppermute | solution.py:26
  52.8 20.5 %collective-permute-start.10 = (bf16[9,10,282]{2,1,0:T(8,128)(2,1)S(1)}, bf16[9,10,282]{2,1,0:T(8,128)(2,1)S(1)}, u32[]{:S(2)}, u32[]{:S(2)}) collective-permute-start(bf16[9,10,282]{2,1,0:T(8,128)(2,1)S(1)} %get-tuple-element.115), channel_id=1, source_target_pairs={{8,0},{16,8},{24,16},{32,24},{40,32},{48,40},{56,48},{64,56},{72,6... | collective-permute-start | bytes 152288 | tf_op jit(solution)/shard_map/ppermute | solution.py:27
  59.7 12.6 %collective-permute-start.5 = (bf16[9,10,282]{2,1,0:T(8,128)(2,1)S(1)}, bf16[9,10,282]{2,1,0:T(8,128)(2,1)S(1)}, u32[]{:S(2)}, u32[]{:S(2)}) collective-permute-start(bf16[9,10,282]{2,1,0:T(8,128)(2,1)S(1)} %get-tuple-element.116), channel_id=1, source_target_pairs={{0,8},{8,16},{16,24},{24,32},{32,40},{40,48},{48,56},{56,64},{64,7... | collective-permute-start | bytes 152288 | tf_op jit(solution)/shard_map/ppermute | solution.py:26
  61.8 12.5 %collective-permute-start.11 = (bf16[9,13,282]{2,1,0:T(8,128)(2,1)S(1)}, bf16[9,13,282]{2,1,0:T(8,128)(2,1)S(1)}, u32[]{:S(2)}, u32[]{:S(2)}) collective-permute-start(bf16[9,13,282]{2,1,0:T(8,128)(2,1)S(1)} %get-tuple-element.113), channel_id=1, source_target_pairs={{8,0},{16,8},{24,16},{32,24},{40,32},{48,40},{56,48},{64,56},{72,6... | collective-permute-start | bytes 197972 | tf_op jit(solution)/shard_map/ppermute | solution.py:27
  68.3 8.8 %collective-permute-start.2 = (bf16[9,13,282]{2,1,0:T(8,128)(2,1)S(1)}, bf16[9,13,282]{2,1,0:T(8,128)(2,1)S(1)}, u32[]{:S(2)}, u32[]{:S(2)}) collective-permute-start(bf16[9,13,282]{2,1,0:T(8,128)(2,1)S(1)} %get-tuple-element.114), channel_id=1, source_target_pairs={{0,8},{8,16},{16,24},{24,32},{32,40},{40,48},{48,56},{56,64},{64,7... | collective-permute-start | bytes 197972 | tf_op jit(solution)/shard_map/ppermute | solution.py:26
  105.2 27.3 %copy-start.3 = (f32[64,256]{1,0:T(8,128)S(1)}, f32[64,256]{1,0:T(8,128)}, u32[]{:S(2)}) copy-start(f32[64,256]{1,0:T(8,128)} %get-tuple-element.31) | copy-start | bytes 196612
  112.4 20.8 %copy-start.4 = (f32[64,256]{1,0:T(8,128)}, f32[64,256]{1,0:T(8,128)S(1)}, u32[]{:S(2)}) copy-start(f32[64,256]{1,0:T(8,128)S(1)} %get-tuple-element.30) | copy-start | bytes 196612
  112.5 6.5 %collective-permute-start.13 = (f32[1,256]{1,0:T(1,128)S(1)}, f32[1,256]{1,0:T(1,128)S(1)}, u32[]{:S(2)}, u32[]{:S(2)}) collective-permute-start(f32[1,256]{1,0:T(1,128)S(1)} %get-tuple-element.221), channel_id=1, source_target_pairs={{8,0},{16,8},{24,16},{32,24},{40,32},{48,40},{56,48},{64,56},{72,6... | collective-permute-start | bytes 3080 | tf_op jit(solution)/shard_map/ppermute | solution.py:27
  117.1 7.6 %collective-permute-start.12 = (f32[1,256]{1,0:T(1,128)S(1)}, f32[1,256]{1,0:T(1,128)S(1)}, u32[]{:S(2)}, u32[]{:S(2)}) collective-permute-start(f32[1,256]{1,0:T(1,128)S(1)} %get-tuple-element.222), channel_id=1, source_target_pairs={{0,8},{8,16},{16,24},{24,32},{32,40},{40,48},{48,56},{56,64},{64,7... | collective-permute-start | bytes 3080 | tf_op jit(solution)/shard_map/ppermute | solution.py:26
  124.7 5.9 %collective-permute-start.14 = (f32[66,1]{1,0:T(8,128)S(1)}, f32[66,1]{1,0:T(8,128)S(1)}, u32[]{:S(2)}, u32[]{:S(2)}) collective-permute-start(f32[66,1]{1,0:T(8,128)S(1)} %get-tuple-element.217), channel_id=1, source_target_pairs={{1,0},{2,1},{3,2},{4,3},{5,4},{6,5},{7,6},{9,8},{10,9},{11,10},{12... | collective-permute-start | bytes 800 | tf_op jit(solution)/shard_map/ppermute | solution.py:27
  126.7 5.9 %collective-permute-start.15 = (f32[66,1]{1,0:T(8,128)S(1)}, f32[66,1]{1,0:T(8,128)S(1)}, u32[]{:S(2)}, u32[]{:S(2)}) collective-permute-start(f32[66,1]{1,0:T(8,128)S(1)} %get-tuple-element.218), channel_id=1, source_target_pairs={{0,1},{1,2},{2,3},{3,4},{4,5},{5,6},{6,7},{8,9},{9,10},{10,11},{11... | collective-permute-start | bytes 800 | tf_op jit(solution)/shard_map/ppermute | solution.py:26
  133.3 43.6 %collective-permute-start.17 = (f32[1,256]{1,0:T(1,128)S(1)}, f32[1,256]{1,0:T(1,128)S(1)}, u32[]{:S(2)}, u32[]{:S(2)}) collective-permute-start(f32[1,256]{1,0:T(1,128)S(1)} %get-tuple-element.219), channel_id=1, source_target_pairs={{8,0},{16,8},{24,16},{32,24},{40,32},{48,40},{56,48},{64,56},{72,6... | collective-permute-start | bytes 3080 | tf_op jit(solution)/shard_map/ppermute | solution.py:27
  135.2 41.7 %collective-permute-start.16 = (f32[1,256]{1,0:T(1,128)S(1)}, f32[1,256]{1,0:T(1,128)S(1)}, u32[]{:S(2)}, u32[]{:S(2)}) collective-permute-start(f32[1,256]{1,0:T(1,128)S(1)} %get-tuple-element.220), channel_id=1, source_target_pairs={{0,8},{8,16},{16,24},{24,32},{32,40},{40,48},{48,56},{56,64},{64,7... | collective-permute-start | bytes 3080 | tf_op jit(solution)/shard_map/ppermute | solution.py:26
  177.0 25.0 %collective-permute-start.18 = (f32[66,1]{1,0:T(8,128)S(1)}, f32[66,1]{1,0:T(8,128)S(1)}, u32[]{:S(2)}, u32[]{:S(2)}) collective-permute-start(f32[66,1]{1,0:T(8,128)S(1)} %get-tuple-element.215), channel_id=1, source_target_pairs={{1,0},{2,1},{3,2},{4,3},{5,4},{6,5},{7,6},{9,8},{10,9},{11,10},{12... | collective-permute-start | bytes 800 | tf_op jit(solution)/shard_map/ppermute | solution.py:27
  185.0 17.1 %collective-permute-start.19 = (f32[66,1]{1,0:T(8,128)S(1)}, f32[66,1]{1,0:T(8,128)S(1)}, u32[]{:S(2)}, u32[]{:S(2)}) collective-permute-start(f32[66,1]{1,0:T(8,128)S(1)} %get-tuple-element.216), channel_id=1, source_target_pairs={{0,1},{1,2},{2,3},{3,4},{4,5},{5,6},{6,7},{8,9},{9,10},{10,11},{11... | collective-permute-start | bytes 800 | tf_op jit(solution)/shard_map/ppermute | solution.py:26
where the time goes:
time: 257 us; the launch traced here: 256 us
  blocking collectives  99.2 us (39%)
  starting transfers between devices  69.9 us (27%)
  other arithmetic  49.4 us (19%)
  local copies, waits for them, and re-layouts  16 us (6%)
  waiting for transfers between devices  14.5 us (6%)
  between operations  7.14 us (3%)
    psum x10, blocking collectives, by_axis(): array = lax.psum(array, axis)  99.2 us
    ppermute x10, starting transfers between devices, with_halo(): after = lax.ppermute(leading, axis, down)  46.2 us
    div x1, other arithmetic, shards(): source = source_sum / VIEWS  27.1 us
    ppermute x10, starting transfers between devices, with_halo(): before = lax.ppermute(last, axis, up)  23.7 us
    ppermute x10, waiting for transfers between devices, with_halo(): before = lax.ppermute(last, axis, up)  14.5 us
    div x1, other arithmetic, shards(): scaled_res = residual / precond  7.21 us
    convert_element_type x9, other arithmetic, shards(): image = band[tindex].astype(jnp.float32)  6.21 us
    unnamed x12, local copies, waits for them, and re-layouts  5.38 us
  transfers between devices with their start and end apart: 20, of which 4 were waited for; matrix products, arithmetic and copies ran while one was open for 5% of the time, Pallas kernels for 0%

commit v1 on v0

--- a/solution.py
+++ b/solution.py
@@ -31,7 +31,7 @@
 
 def by_axis(array, axes):
     for axis in axes:
-        array = lax.psum(array, axis)
+        array = jnp.sum(lax.all_gather(array, axis), axis=0)
     return array
 
 

time: 257 us -> 293 us (1.14)
  local copies, waits for them, and re-layouts: 16 us -> 48.8 us
  other arithmetic: 49.4 us -> 64.8 us
  starting transfers between devices: 69.9 us -> 61.7 us
  waiting for transfers between devices: 14.5 us -> 6.51 us
    unnamed x0 -> x10, blocking collectives: none -> 101 us
    psum x10 -> x0, blocking collectives: 99.2 us -> none  [by_axis(): array = lax.psum(array, axis)]
    unnamed x12 -> x53, local copies, waits for them, and re-layouts: 5.38 us -> 38.3 us
    ppermute x10, starting transfers between devices: 46.2 us -> 33.6 us  [with_halo(): after = lax.ppermute(leading, axis, down)]
    reduce_sum x0 -> x20, other arithmetic: none -> 12.5 us  [by_axis(): array = jnp.sum(lax.all_gather(array, axis), axis=0)]
    ppermute x10, waiting for transfers between devices: 14.5 us -> 3.71 us  [with_halo(): before = lax.ppermute(last, axis, up)]
    ppermute x10, starting transfers between devices: 23.7 us -> 28.1 us  [with_halo(): before = lax.ppermute(last, axis, up)]
  transfers between devices with their start and end apart: 20 -> 20, of which waited for: 4 -> 5; matrix products, arithmetic and copies ran while one was open for 5% -> 11% of each run, Pallas kernels for 0% -> 0%
where the time goes in v1:
time: 293 us; the launch traced here: 290 us
  blocking collectives  101 us (34%)
  other arithmetic  64.8 us (22%)
  starting transfers between devices  61.7 us (21%)
  local copies, waits for them, and re-layouts  48.8 us (17%)
  between operations  7.15 us (2%)
  waiting for transfers between devices  6.51 us (2%)
    unnamed x10, blocking collectives  101 us
    unnamed x53, local copies, waits for them, and re-layouts  38.3 us
    ppermute x10, starting transfers between devices, with_halo(): after = lax.ppermute(leading, axis, down)  33.6 us
    ppermute x10, starting transfers between devices, with_halo(): before = lax.ppermute(last, axis, up)  28.1 us
    div x1, other arithmetic, shards(): source = source_sum / VIEWS  27 us
    reduce_sum x20, other arithmetic, by_axis(): array = jnp.sum(lax.all_gather(array, axis), axis=0)  12.5 us
    div x1, other arithmetic, shards(): scaled_res = residual / precond  7.86 us
    convert_element_type x9, other arithmetic, shards(): image = band[tindex].astype(jnp.float32)  6.25 us
  transfers between devices with their start and end apart: 20, of which 5 were waited for; matrix products, arithmetic and copies ran while one was open for 11% of the time, Pallas kernels for 0%

profile of v1, /device:TPU:10, one launch (start us, length us, event | category | flops | bytes accessed | tf_op | source)
XLA Modules:
  0.0 289.8 jit_solution(322235027046883568)
XLA Ops:
  0.6 3.4 %fusion.427 = (bf16[81,64,13]{2,1,0:T(8,128)(2,1)S(1)}, bf16[81,64,13]{2,1,0:T(8,128)(2,1)}) fusion(bf16[81,64,256]{2,1,0:T(8,128)(2,1)} %param.1), kind=kLoop, calls=%fused_computation.861 | loop fusion | bytes 539136 | tf_op jit(solution)/shard_map/slice | solution.py:24
  5.8 3.7 %collective-permute-start = (bf16[81,64,13]{0,1,2:T(8,128)(2,1)S(1)}, bf16[81,64,13]{0,1,2:T(8,128)(2,1)S(1)}, u32[]{:S(2)}, u32[]{:S(2)}) collective-permute-start(bf16[81,64,13]{0,1,2:T(8,128)(2,1)S(1)} %copy.7), channel_id=1, source_target_pairs={{0,1},{1,2},{2,3},{3,4},{4,5},{5,6},{6,7},{8,9},{9,10},{10,11},{11... | collective-permute-start | bytes 404360 | tf_op jit(solution)/shard_map/ppermute | solution.py:26
  9.4 2.9 copy.8
  12.3 2.5 collective-permute-start.1
  14.9 3.2 %copy.5 = bf16[81,64,13]{2,1,0:T(8,128)(2,1)} copy(bf16[81,64,13]{0,1,2:T(8,128)(2,1)S(1)} %collective-permute-done) | data formatting | bytes 269568 | tf_op jit(solution)/shard_map/ppermute | solution.py:26
  18.1 2.8 collective-permute-done.1
  20.9 3.2 %copy.6 = bf16[81,64,13]{2,1,0:T(8,128)(2,1)} copy(bf16[81,64,13]{0,1,2:T(8,128)(2,1)S(1)} %collective-permute-done.1) | data formatting | bytes 269568 | tf_op jit(solution)/shard_map/ppermute | solution.py:27
  24.1 4.3 %pad_maximum_fusion = bf16[81,64,282]{2,1,0:T(8,128)(2,1)S(1)} fusion(bf16[81,64,13]{2,1,0:T(8,128)(2,1)} %copy.6, bf16[81,64,256]{2,1,0:T(8,128)(2,1)S(1)} %copy-done, bf16[81,64,13]{2,1,0:T(8,128)(2,1)} %copy.5), kind=kLoop, calls=%fused_computation | loop fusion | flops 8771328 | bytes 5847552 | tf_op jit(solution)/shard_map/concatenate | solution.py:28
  31.5 6.3 %collective-permute-start.4 = (bf16[9,1,282]{2,1,0:T(2,128)(2,1)S(1)}, bf16[9,1,282]{2,1,0:T(2,128)(2,1)S(1)}, u32[]{:S(2)}, u32[]{:S(2)}) collective-permute-start(bf16[9,1,282]{2,1,0:T(2,128)(2,1)S(1)} %get-tuple-element.122), channel_id=1, source_target_pairs={{8,0},{16,8},{24,16},{32,24},{40,32},{48,40},{56,48},{64,56},{72,6... | collective-permute-start | bytes 15236 | tf_op jit(solution)/shard_map/ppermute | solution.py:27
  37.9 2.1 collective-permute-start.11
  40.0 3.6 %collective-permute-start.10 = (bf16[9,10,282]{2,1,0:T(8,128)(2,1)S(1)}, bf16[9,10,282]{2,1,0:T(8,128)(2,1)S(1)}, u32[]{:S(2)}, u32[]{:S(2)}) collective-permute-start(bf16[9,10,282]{2,1,0:T(8,128)(2,1)S(1)} %get-tuple-element.115), channel_id=1, source_target_pairs={{8,0},{16,8},{24,16},{32,24},{40,32},{48,40},{56,48},{64,56},{72,6... | collective-permute-start | bytes 152288 | tf_op jit(solution)/shard_map/ppermute | solution.py:27
  45.6 2.1 collective-permute-start.8
  47.8 2.2 collective-permute-start.7
  50.6 3.6 %collective-permute-start.6 = (bf16[9,7,282]{2,1,0:T(8,128)(2,1)S(1)}, bf16[9,7,282]{2,1,0:T(8,128)(2,1)S(1)}, u32[]{:S(2)}, u32[]{:S(2)}) collective-permute-start(bf16[9,7,282]{2,1,0:T(8,128)(2,1)S(1)} %get-tuple-element.118), channel_id=1, source_target_pairs={{0,8},{8,16},{16,24},{24,32},{32,40},{40,48},{48,56},{56,64},{64,7... | collective-permute-start | bytes 106604 | tf_op jit(solution)/shard_map/ppermute | solution.py:26
  67.4 27.0 %subtract_multiply_fusion = (f32[64,256]{1,0:T(8,128)}, f32[64,256]{1,0:T(8,128)}, f32[64,256]{1,0:T(8,128)}, f32[64,256]{1,0:T(8,128)}, f32[64,256]{1,0:T(8,128...) fusion(f32[66,282]{1,0:T(8,128)} %get-tuple-element.169, ...), kind=kLoop, calls=%fused_computation.594 | loop fusion | flops 14188544 | bytes 31981568 | tf_op jit(solution)/shard_map/div | solution.py:90
  94.4 7.9 %fusion.344 = (f32[64,256]{1,0:T(8,128)S(1)}, f32[64,256]{1,0:T(8,128)}, f32[64,256]{1,0:T(8,128)}) fusion(f32[64,256]{1,0:T(8,128)} %get-tuple-element.31, f32[65,256]{1,0:T(8,128)S(1)} %fusion.3, f32[64,257]{1,0:T(8,128)S(1)} %fusion.1, f32[64,256]{1,0:T(8,128)} %get-tuple-element.112, f32[66,282]{1,0:T(8,128)} %get-tuple-element.134, ...), kind=kLoop, calls=%fused_computation.859 | loop fusion | flops 8077312 | bytes 11206656 | tf_op jit(solution)/shard_map/div | solution.py:106
  104.2 6.3 %collective-permute-start.13 = (f32[1,256]{1,0:T(1,128)S(1)}, f32[1,256]{1,0:T(1,128)S(1)}, u32[]{:S(2)}, u32[]{:S(2)}) collective-permute-start(f32[1,256]{1,0:T(1,128)S(1)} %get-tuple-element.221), channel_id=1, source_target_pairs={{8,0},{16,8},{24,16},{32,24},{40,32},{48,40},{56,48},{64,56},{72,6... | collective-permute-start | bytes 3080 | tf_op jit(solution)/shard_map/ppermute | solution.py:27
  113.2 2.4 collective-permute-start.14
  115.7 6.1 %collective-permute-start.15 = (f32[66,1]{1,0:T(8,128)S(1)}, f32[66,1]{1,0:T(8,128)S(1)}, u32[]{:S(2)}, u32[]{:S(2)}) collective-permute-start(f32[66,1]{1,0:T(8,128)S(1)} %get-tuple-element.218), channel_id=1, source_target_pairs={{0,1},{1,2},{2,3},{3,4},{4,5},{5,6},{6,7},{8,9},{9,10},{10,11},{11... | collective-permute-start | bytes 800 | tf_op jit(solution)/shard_map/ppermute | solution.py:26
  129.7 8.7 %all-reduce.25 = (f32[4]{0:T(128)S(1)}, f32[4]{0:T(128)S(1)}) all-reduce(f32[4]{0:T(128)S(1)} %dynamic-update-slice, f32[4]{0:T(128)S(1)} %dynamic-update-slice.5), channel_id=1, replica_groups=mesh['row_0'=4,'row_1'=4,'row_2'=2,'col_0'=2,'col_1'=4] {'row_0'}, use_global_device_ids=true, to_apply=%add | all-reduce | flops 8 | bytes 64
  144.3 9.6 %all-reduce.23 = (f32[4]{0:T(128)S(1)}, f32[4]{0:T(128)S(1)}) all-reduce(f32[4]{0:T(128)S(1)} %dynamic-update-slice.1, f32[4]{0:T(128)S(1)} %dynamic-update-slice.6), channel_id=1, replica_groups=mesh['row_0'=4,'row_1'=4,'row_2'=2,'col_0'=2,'col_1'=4] {'row_1'}, use_global_device_ids=true, to_apply=%add.1 | all-reduce | flops 8 | bytes 64
  157.8 3.1 %collective-permute-start.17 = (f32[1,256]{1,0:T(1,128)S(1)}, f32[1,256]{1,0:T(1,128)S(1)}, u32[]{:S(2)}, u32[]{:S(2)}) collective-permute-start(f32[1,256]{1,0:T(1,128)S(1)} %get-tuple-element.219), channel_id=1, source_target_pairs={{8,0},{16,8},{24,16},{32,24},{40,32},{48,40},{56,48},{64,56},{72,6... | collective-permute-start | bytes 3080 | tf_op jit(solution)/shard_map/ppermute | solution.py:27
  160.9 2.6 all-reduce.29
  168.9 20.6 %all-reduce.27 = (f32[2]{0:T(128)S(1)}, f32[2]{0:T(128)S(1)}) all-reduce(f32[2]{0:T(128)S(1)} %dynamic-update-slice.3, f32[2]{0:T(128)S(1)} %dynamic-update-slice.8), channel_id=1, replica_groups=mesh['row_0'=4,'row_1'=4,'row_2'=2,'col_0'=2,'col_1'=4] {'col_0'}, use_global_device_ids=true, to_apply=%add.3 | all-reduce | flops 4 | bytes 32
  193.5 15.7 %all-reduce.21 = (f32[4]{0:T(128)S(1)}, f32[4]{0:T(128)S(1)}) all-reduce(f32[4]{0:T(128)S(1)} %dynamic-update-slice.4, f32[4]{0:T(128)S(1)} %dynamic-update-slice.9), channel_id=1, replica_groups=mesh['row_0'=4,'row_1'=4,'row_2'=2,'col_0'=2,'col_1'=4] {'col_1'}, use_global_device_ids=true, to_apply=%add.4 | all-reduce | flops 8 | bytes 64
  209.4 3.2 %collective-permute-start.18 = (f32[66,1]{1,0:T(8,128)S(1)}, f32[66,1]{1,0:T(8,128)S(1)}, u32[]{:S(2)}, u32[]{:S(2)}) collective-permute-start(f32[66,1]{1,0:T(8,128)S(1)} %get-tuple-element.215), channel_id=1, source_target_pairs={{1,0},{2,1},{3,2},{4,3},{5,4},{6,5},{7,6},{9,8},{10,9},{11,10},{12... | collective-permute-start | bytes 800 | tf_op jit(solution)/shard_map/ppermute | solution.py:27
  212.5 2.7 collective-permute-start.19
  222.8 8.5 %all-reduce.24 = (f32[4]{0:T(128)S(1)}, f32[4]{0:T(128)S(1)}) all-reduce(f32[4]{0:T(128)S(1)} %dynamic-update-slice.10, f32[4]{0:T(128)S(1)} %dynamic-update-slice.15), channel_id=1, replica_groups=mesh['row_0'=4,'row_1'=4,'row_2'=2,'col_0'=2,'col_1'=4] {'row_0'}, use_global_device_ids=true, to_apply=%add.10 | all-reduce | flops 8 | bytes 64
  235.2 9.9 %all-reduce.22 = (f32[4]{0:T(128)S(1)}, f32[4]{0:T(128)S(1)}) all-reduce(f32[4]{0:T(128)S(1)} %dynamic-update-slice.11, f32[4]{0:T(128)S(1)} %dynamic-update-slice.16), channel_id=1, replica_groups=mesh['row_0'=4,'row_1'=4,'row_2'=2,'col_0'=2,'col_1'=4] {'row_1'}, use_global_device_ids=true, to_apply=%add.11 | all-reduce | flops 8 | bytes 64
  248.9 2.4 all-reduce.28
  255.3 8.8 %all-reduce.26 = (f32[2]{0:T(128)S(1)}, f32[2]{0:T(128)S(1)}) all-reduce(f32[2]{0:T(128)S(1)} %dynamic-update-slice.13, f32[2]{0:T(128)S(1)} %dynamic-update-slice.18), channel_id=1, replica_groups=mesh['row_0'=4,'row_1'=4,'row_2'=2,'col_0'=2,'col_1'=4] {'col_0'}, use_global_device_ids=true, to_apply=%add.13 | all-reduce | flops 4 | bytes 32
  268.4 13.9 %all-reduce.20 = (f32[4]{0:T(128)S(1)}, f32[4]{0:T(128)S(1)}) all-reduce(f32[4]{0:T(128)S(1)} %dynamic-update-slice.14, f32[4]{0:T(128)S(1)} %dynamic-update-slice.19), channel_id=1, replica_groups=mesh['row_0'=4,'row_1'=4,'row_2'=2,'col_0'=2,'col_1'=4] {'col_1'}, use_global_device_ids=true, to_apply=%add.14 | all-reduce | flops 8 | bytes 64
  (128 shorter events, 77.2 us)
Async XLA Ops:
  5.8 18.4 %copy-start = (bf16[81,64,256]{2,1,0:T(8,128)(2,1)S(1)}, bf16[81,64,256]{2,1,0:T(8,128)(2,1)}, u32[]{:S(2)}) copy-start(bf16[81,64,256]{2,1,0:T(8,128)(2,1)} %param.1) | copy-start | bytes 7962628
  5.8 9.1 %collective-permute-start = (bf16[81,64,13]{0,1,2:T(8,128)(2,1)S(1)}, bf16[81,64,13]{0,1,2:T(8,128)(2,1)S(1)}, u32[]{:S(2)}, u32[]{:S(2)}) collective-permute-start(bf16[81,64,13]{0,1,2:T(8,128)(2,1)S(1)} %copy.7), channel_id=1, source_target_pairs={{0,1},{1,2},{2,3},{3,4},{4,5},{5,6},{6,7},{8,9},{9,10},{10,11},{11... | collective-permute-start | bytes 404360 | tf_op jit(solution)/shard_map/ppermute | solution.py:26
  12.3 8.6 %collective-permute-start.1 = (bf16[81,64,13]{0,1,2:T(8,128)(2,1)S(1)}, bf16[81,64,13]{0,1,2:T(8,128)(2,1)S(1)}, u32[]{:S(2)}, u32[]{:S(2)}) collective-permute-start(bf16[81,64,13]{0,1,2:T(8,128)(2,1)S(1)} %copy.8), channel_id=1, source_target_pairs={{1,0},{2,1},{3,2},{4,3},{5,4},{6,5},{7,6},{9,8},{10,9},{11,10},{12... | collective-permute-start | bytes 404360 | tf_op jit(solution)/shard_map/ppermute | solution.py:27
  24.1 4.3 %copy-start.1 = (bf16[81,64,13]{2,1,0:T(8,128)(2,1)S(1)}, bf16[81,64,13]{2,1,0:T(8,128)(2,1)}, u32[]{:S(2)}) copy-start(bf16[81,64,13]{2,1,0:T(8,128)(2,1)} %copy.5) | copy-start | bytes 404356
  24.1 4.3 %copy-start.2 = (bf16[81,64,13]{2,1,0:T(8,128)(2,1)S(1)}, bf16[81,64,13]{2,1,0:T(8,128)(2,1)}, u32[]{:S(2)}) copy-start(bf16[81,64,13]{2,1,0:T(8,128)(2,1)} %copy.6) | copy-start | bytes 404356
  29.5 16.1 %collective-permute-start.3 = (bf16[9,1,282]{2,1,0:T(2,128)(2,1)S(1)}, bf16[9,1,282]{2,1,0:T(2,128)(2,1)S(1)}, u32[]{:S(2)}, u32[]{:S(2)}) collective-permute-start(bf16[9,1,282]{2,1,0:T(2,128)(2,1)S(1)} %get-tuple-element.121), channel_id=1, source_target_pairs={{0,8},{8,16},{16,24},{24,32},{32,40},{40,48},{48,56},{56,64},{64,7... | collective-permute-start | bytes 15236 | tf_op jit(solution)/shard_map/ppermute | solution.py:26
  31.5 16.3 %collective-permute-start.4 = (bf16[9,1,282]{2,1,0:T(2,128)(2,1)S(1)}, bf16[9,1,282]{2,1,0:T(2,128)(2,1)S(1)}, u32[]{:S(2)}, u32[]{:S(2)}) collective-permute-start(bf16[9,1,282]{2,1,0:T(2,128)(2,1)S(1)} %get-tuple-element.122), channel_id=1, source_target_pairs={{8,0},{16,8},{24,16},{32,24},{40,32},{48,40},{56,48},{64,56},{72,6... | collective-permute-start | bytes 15236 | tf_op jit(solution)/shard_map/ppermute | solution.py:27
  37.9 27.5 %collective-permute-start.11 = (bf16[9,13,282]{2,1,0:T(8,128)(2,1)S(1)}, bf16[9,13,282]{2,1,0:T(8,128)(2,1)S(1)}, u32[]{:S(2)}, u32[]{:S(2)}) collective-permute-start(bf16[9,13,282]{2,1,0:T(8,128)(2,1)S(1)} %get-tuple-element.113), channel_id=1, source_target_pairs={{8,0},{16,8},{24,16},{32,24},{40,32},{48,40},{56,48},{64,56},{72,6... | collective-permute-start | bytes 197972 | tf_op jit(solution)/shard_map/ppermute | solution.py:27
  40.0 21.7 %collective-permute-start.10 = (bf16[9,10,282]{2,1,0:T(8,128)(2,1)S(1)}, bf16[9,10,282]{2,1,0:T(8,128)(2,1)S(1)}, u32[]{:S(2)}, u32[]{:S(2)}) collective-permute-start(bf16[9,10,282]{2,1,0:T(8,128)(2,1)S(1)} %get-tuple-element.115), channel_id=1, source_target_pairs={{8,0},{16,8},{24,16},{32,24},{40,32},{48,40},{56,48},{64,56},{72,6... | collective-permute-start | bytes 152288 | tf_op jit(solution)/shard_map/ppermute | solution.py:27
  43.7 14.0 %collective-permute-start.9 = (bf16[9,7,282]{2,1,0:T(8,128)(2,1)S(1)}, bf16[9,7,282]{2,1,0:T(8,128)(2,1)S(1)}, u32[]{:S(2)}, u32[]{:S(2)}) collective-permute-start(bf16[9,7,282]{2,1,0:T(8,128)(2,1)S(1)} %get-tuple-element.117), channel_id=1, source_target_pairs={{8,0},{16,8},{24,16},{32,24},{40,32},{48,40},{56,48},{64,56},{72,6... | collective-permute-start | bytes 106604 | tf_op jit(solution)/shard_map/ppermute | solution.py:27
  45.6 4.9 %collective-permute-start.8 = (bf16[9,4,282]{2,1,0:T(4,128)(2,1)S(1)}, bf16[9,4,282]{2,1,0:T(4,128)(2,1)S(1)}, u32[]{:S(2)}, u32[]{:S(2)}) collective-permute-start(bf16[9,4,282]{2,1,0:T(4,128)(2,1)S(1)} %get-tuple-element.119), channel_id=1, source_target_pairs={{8,0},{16,8},{24,16},{32,24},{40,32},{48,40},{56,48},{64,56},{72,6... | collective-permute-start | bytes 60920 | tf_op jit(solution)/shard_map/ppermute | solution.py:27
  47.8 7.9 %collective-permute-start.7 = (bf16[9,4,282]{2,1,0:T(4,128)(2,1)S(1)}, bf16[9,4,282]{2,1,0:T(4,128)(2,1)S(1)}, u32[]{:S(2)}, u32[]{:S(2)}) collective-permute-start(bf16[9,4,282]{2,1,0:T(4,128)(2,1)S(1)} %get-tuple-element.120), channel_id=1, source_target_pairs={{0,8},{8,16},{16,24},{24,32},{32,40},{40,48},{48,56},{56,64},{64,7... | collective-permute-start | bytes 60920 | tf_op jit(solution)/shard_map/ppermute | solution.py:26
  50.6 10.2 %collective-permute-start.6 = (bf16[9,7,282]{2,1,0:T(8,128)(2,1)S(1)}, bf16[9,7,282]{2,1,0:T(8,128)(2,1)S(1)}, u32[]{:S(2)}, u32[]{:S(2)}) collective-permute-start(bf16[9,7,282]{2,1,0:T(8,128)(2,1)S(1)} %get-tuple-element.118), channel_id=1, source_target_pairs={{0,8},{8,16},{16,24},{24,32},{32,40},{40,48},{48,56},{56,64},{64,7... | collective-permute-start | bytes 106604 | tf_op jit(solution)/shard_map/ppermute | solution.py:26
  55.6 8.8 %collective-permute-start.5 = (bf16[9,10,282]{2,1,0:T(8,128)(2,1)S(1)}, bf16[9,10,282]{2,1,0:T(8,128)(2,1)S(1)}, u32[]{:S(2)}, u32[]{:S(2)}) collective-permute-start(bf16[9,10,282]{2,1,0:T(8,128)(2,1)S(1)} %get-tuple-element.116), channel_id=1, source_target_pairs={{0,8},{8,16},{16,24},{24,32},{32,40},{40,48},{48,56},{56,64},{64,7... | collective-permute-start | bytes 152288 | tf_op jit(solution)/shard_map/ppermute | solution.py:26
  57.7 8.8 %collective-permute-start.2 = (bf16[9,13,282]{2,1,0:T(8,128)(2,1)S(1)}, bf16[9,13,282]{2,1,0:T(8,128)(2,1)S(1)}, u32[]{:S(2)}, u32[]{:S(2)}) collective-permute-start(bf16[9,13,282]{2,1,0:T(8,128)(2,1)S(1)} %get-tuple-element.114), channel_id=1, source_target_pairs={{0,8},{8,16},{16,24},{24,32},{32,40},{40,48},{48,56},{56,64},{64,7... | collective-permute-start | bytes 197972 | tf_op jit(solution)/shard_map/ppermute | solution.py:26
  102.3 10.9 %collective-permute-start.12 = (f32[1,256]{1,0:T(1,128)S(1)}, f32[1,256]{1,0:T(1,128)S(1)}, u32[]{:S(2)}, u32[]{:S(2)}) collective-permute-start(f32[1,256]{1,0:T(1,128)S(1)} %get-tuple-element.222), channel_id=1, source_target_pairs={{0,8},{8,16},{16,24},{24,32},{32,40},{40,48},{48,56},{56,64},{64,7... | collective-permute-start | bytes 3080 | tf_op jit(solution)/shard_map/ppermute | solution.py:26
  104.2 8.9 %collective-permute-start.13 = (f32[1,256]{1,0:T(1,128)S(1)}, f32[1,256]{1,0:T(1,128)S(1)}, u32[]{:S(2)}, u32[]{:S(2)}) collective-permute-start(f32[1,256]{1,0:T(1,128)S(1)} %get-tuple-element.221), channel_id=1, source_target_pairs={{8,0},{16,8},{24,16},{32,24},{40,32},{48,40},{56,48},{64,56},{72,6... | collective-permute-start | bytes 3080 | tf_op jit(solution)/shard_map/ppermute | solution.py:27
  113.2 11.2 %collective-permute-start.14 = (f32[66,1]{1,0:T(8,128)S(1)}, f32[66,1]{1,0:T(8,128)S(1)}, u32[]{:S(2)}, u32[]{:S(2)}) collective-permute-start(f32[66,1]{1,0:T(8,128)S(1)} %get-tuple-element.217), channel_id=1, source_target_pairs={{1,0},{2,1},{3,2},{4,3},{5,4},{6,5},{7,6},{9,8},{10,9},{11,10},{12... | collective-permute-start | bytes 800 | tf_op jit(solution)/shard_map/ppermute | solution.py:27
  115.7 8.8 %collective-permute-start.15 = (f32[66,1]{1,0:T(8,128)S(1)}, f32[66,1]{1,0:T(8,128)S(1)}, u32[]{:S(2)}, u32[]{:S(2)}) collective-permute-start(f32[66,1]{1,0:T(8,128)S(1)} %get-tuple-element.218), channel_id=1, source_target_pairs={{0,1},{1,2},{2,3},{3,4},{4,5},{5,6},{6,7},{8,9},{9,10},{10,11},{11... | collective-permute-start | bytes 800 | tf_op jit(solution)/shard_map/ppermute | solution.py:26
  142.4 66.9 %collective-permute-start.16 = (f32[1,256]{1,0:T(1,128)S(1)}, f32[1,256]{1,0:T(1,128)S(1)}, u32[]{:S(2)}, u32[]{:S(2)}) collective-permute-start(f32[1,256]{1,0:T(1,128)S(1)} %get-tuple-element.220), channel_id=1, source_target_pairs={{0,8},{8,16},{16,24},{24,32},{32,40},{40,48},{48,56},{56,64},{64,7... | collective-permute-start | bytes 3080 | tf_op jit(solution)/shard_map/ppermute | solution.py:26
  157.8 51.5 %collective-permute-start.17 = (f32[1,256]{1,0:T(1,128)S(1)}, f32[1,256]{1,0:T(1,128)S(1)}, u32[]{:S(2)}, u32[]{:S(2)}) collective-permute-start(f32[1,256]{1,0:T(1,128)S(1)} %get-tuple-element.219), channel_id=1, source_target_pairs={{8,0},{16,8},{24,16},{32,24},{40,32},{48,40},{56,48},{64,56},{72,6... | collective-permute-start | bytes 3080 | tf_op jit(solution)/shard_map/ppermute | solution.py:27
  209.4 8.4 %collective-permute-start.18 = (f32[66,1]{1,0:T(8,128)S(1)}, f32[66,1]{1,0:T(8,128)S(1)}, u32[]{:S(2)}, u32[]{:S(2)}) collective-permute-start(f32[66,1]{1,0:T(8,128)S(1)} %get-tuple-element.215), channel_id=1, source_target_pairs={{1,0},{2,1},{3,2},{4,3},{5,4},{6,5},{7,6},{9,8},{10,9},{11,10},{12... | collective-permute-start | bytes 800 | tf_op jit(solution)/shard_map/ppermute | solution.py:27
  212.5 5.9 %collective-permute-start.19 = (f32[66,1]{1,0:T(8,128)S(1)}, f32[66,1]{1,0:T(8,128)S(1)}, u32[]{:S(2)}, u32[]{:S(2)}) collective-permute-start(f32[66,1]{1,0:T(8,128)S(1)} %get-tuple-element.216), channel_id=1, source_target_pairs={{0,1},{1,2},{2,3},{3,4},{4,5},{5,6},{6,7},{8,9},{9,10},{10,11},{11... | collective-permute-start | bytes 800 | tf_op jit(solution)/shard_map/ppermute | solution.py:26
